TPU v7x, 256 devices: a whole 4x4x8 slice. The times are simulated.
256 devices in a mesh: grp: 32 (over z, y), tp: 8 (over x, core).
Axes of the slice: x: 4, y: 4, z: 8, core: 2. Of those that a mesh axis runs over, the one named last changes fastest.
Arguments:
- queries: bfloat16 [32, 64, 128], P('grp', 'tp'), may hold values from -12 to 12
- new_keys: bfloat16 [32, 8, 128], P('grp', 'tp'), may hold values from -6 to 6
- new_values: bfloat16 [32, 8, 128], P('grp', 'tp'), may hold values from -6 to 6
- key_cache: bfloat16 [3072, 8, 256, 128], P('grp', 'tp'), may hold values from -6 to 6
- paged_value_cache: bfloat16 [3072, 8, 256, 128], P('grp', 'tp'), may hold values from -6 to 6
- lengths: int32 [32], replicated, may hold values from 1 to 36864, as said below
- placement: int32 [3072, 2], P('grp'), may hold values from 0 to 143, as said below
- out_weight: bfloat16 [8192, 8192], P('tp', 'grp'), may hold values from -0.1875 to 0.1875
Outputs:
- projected: bfloat16 [32, 8192], P(None, ('grp', 'tp'))
Inputs may be any that keep to these rules, and one draw needn't show every extreme that they name: Request r's blocks are numbered 0 to ceil(lengths[r] / 256) - 1. `placement`: row i is slot i, rows of group g being g * 96 to (g + 1) * 96 - 1; first column: the owning request, 32 for an empty slot; second column: the block's number (0 in an empty slot); every block of every request stands in exactly one slot.
All inputs are finite; a program needn't handle non-finite values.
Results may differ from a plain program's by a relative error of at most 0.0048.
Values may be sent and summed in bfloat16 or wider, within the bound.
A program may use at most 64 MiB of HBM per device.

v0:
```python
import jax
import jax.numpy as jnp
from jax import lax
from jax.sharding import PartitionSpec as P

very_negative = -1e30


def slot_terms(q_all, keys, value_rows, placement, lengths):
    req_count = q_all.shape[0]
    slot_count, kv_heads, block_len, head_dim = keys.shape
    group_size = q_all.shape[1] // kv_heads
    score_scale = head_dim ** (-0.5)
    owner_groups = placement[:, 0]
    block_numbers = placement[:, 1]
    onehot = owner_groups[:, None] == jnp.arange(req_count, dtype=jnp.int32)[None, :]
    picked = jnp.dot(
        onehot.astype(jnp.bfloat16),
        q_all.reshape(req_count, -1),
        preferred_element_type=jnp.float32,
    )
    picked = picked.astype(jnp.bfloat16).reshape(slot_count, kv_heads, group_size, head_dim)
    clamped = jnp.minimum(owner_groups, req_count - 1)
    live_len = jnp.take(lengths, clamped)
    positions = block_numbers[:, None] * block_len + jnp.arange(block_len, dtype=jnp.int32)[None, :]
    live_mask = (positions < live_len[:, None]) & (owner_groups < req_count)[:, None]
    scores = (
        jnp.einsum("skgd,skbd->skgb", picked, keys, preferred_element_type=jnp.float32)
        * score_scale
    )
    scores = jnp.where(live_mask[:, None, None, :], scores, very_negative)
    maxima = jnp.max(scores, -1)
    weights = jnp.exp(scores - maxima[..., None]) * live_mask[:, None, None, :].astype(jnp.float32)
    totals = jnp.sum(weights, -1)
    mixture = jnp.einsum(
        "skgb,skbd->skgd",
        weights.astype(jnp.bfloat16),
        value_rows,
        preferred_element_type=jnp.float32,
    )
    best = jnp.max(jnp.where(onehot[:, :, None, None], maxima[:, None], very_negative), 0)
    factor = jnp.exp(maxima - jnp.take(best, clamped, axis=0)) * (owner_groups < req_count)[
        :, None, None
    ].astype(jnp.float32)
    onef = onehot.astype(jnp.float32)
    weight_sum = jnp.einsum("sr,skg->rkg", onef, totals * factor, precision=lax.Precision.HIGHEST)
    value_sum = jnp.einsum(
        "sr,skgd->rkgd", onef, mixture * factor[..., None], precision=lax.Precision.HIGHEST
    )
    return (best, weight_sum, value_sum)


def body(
    queries, new_keys, new_values, key_cache, paged_value_cache, lengths, placement, out_weight
):
    home_rows, head_count, head_dim = queries.shape
    kv_heads = key_cache.shape[1]
    group_size = head_count // kv_heads
    q_all = lax.all_gather(queries, "grp", axis=0, tiled=True)
    best, weight_sum, value_sum = slot_terms(
        q_all, key_cache, paged_value_cache, placement, lengths
    )
    local_q = queries.reshape(home_rows, kv_heads, group_size, head_dim)
    new_score = jnp.einsum(
        "rkgd,rkd->rkg", local_q, new_keys, preferred_element_type=jnp.float32
    ) * head_dim ** (-0.5)
    own_values = new_values[:, :, None, :].astype(jnp.float32)
    maxima, totals, sums = (
        lax.all_to_all(best[:, None], "grp", split_axis=0, concat_axis=1, tiled=True),
        lax.all_to_all(weight_sum[:, None], "grp", split_axis=0, concat_axis=1, tiled=True),
        lax.all_to_all(value_sum[:, None], "grp", split_axis=0, concat_axis=1, tiled=True),
    )
    summit = jnp.maximum(jnp.max(maxima, 1), new_score)
    scaled = jnp.exp(maxima - summit[:, None])
    own_term = jnp.exp(new_score - summit)
    total = jnp.sum(totals * scaled, 1) + own_term
    summed = jnp.sum(sums * scaled[..., None], 1) + own_term[..., None] * own_values
    attention = (
        (summed / total[..., None]).reshape(home_rows, head_count * head_dim).astype(jnp.bfloat16)
    )
    partial_cols = jnp.dot(
        lax.all_gather(attention, "grp", axis=0, tiled=True),
        out_weight,
        preferred_element_type=jnp.float32,
    )
    return lax.psum_scatter(partial_cols, "tp", scatter_dimension=1, tiled=True).astype(
        jnp.bfloat16
    )


def solution(mesh):
    in_specs = (
        P("grp", "tp", None),
        P("grp", "tp", None),
        P("grp", "tp", None),
        P("grp", "tp", None, None),
        P("grp", "tp", None, None),
        P(),
        P("grp", None),
        P("tp", "grp"),
    )
    out_specs = P(None, ("grp", "tp"))
    return jax.shard_map(body, mesh=mesh, in_specs=in_specs, out_specs=out_specs, check_vma=False)
```

profile of v0, /device:TPU:1, one launch (start us, length us, event | category | flops | bytes accessed | tf_op | source)
XLA Modules:
  0.0 194.3 jit_solution(778689192660500160)
XLA Ops:
  6.5 0.0 copy-start
  6.5 0.0 copy-start.2
  6.5 0.8 fusion.36
  7.3 0.7 compare_bitcast_fusion
  8.0 40.5 %all_gather.6 = bf16[32,8,128]{2,1,0:T(8,128)(2,1)S(1)} all-gather(bf16[1,8,128]{2,1,0:T(8,128)(2,1)} %param.8), channel_id=1, replica_groups=mesh['grp'=32,'tp'=8] {'grp'}, dimensions={0}, use_global_device_ids=true | all-gather | bytes 67584 | tf_op jit(solution)/shard_map/all_gather | solution.py:59
  48.5 1.6 gather_fusion
  50.1 0.8 fusion.35
  50.9 0.2 fusion.13
  51.2 0.1 fusion.37
  51.3 4.6 %fusion.39 = (f32[96,8]{1,0:T(8,128)S(1)}, f32[96,8,256]{2,1,0:T(8,128)S(1)}) fusion(bf16[96,8,128]{2,1,0:T(8,128)(2,1)S(1)} %bitcast.88, bf16[96,1,256,128]{3,2,1,0:T(8,128)(2,1)} %param.11, pred[96,256]{1,0:T(8,128)(4,1)S(1)} %get-tuple-element.10), kind=kOutput, calls=%fused_computation.58 | convolution fusion | flops 50920704 | bytes 7302144 | tf_op jit(solution)/shard_map/skgd,skbd->skgb/dot_general | solution.py:28
  55.9 0.0 copy-start.3
  55.9 0.0 copy-start.1
  55.9 0.0 copy-start.4
  55.9 0.1 copy.20
  55.9 0.7 select_reduce_fusion
  56.7 5.9 %all-to-all-start.1 = ((f32[32,1,1,8]{3,2,1,0:T(1,128)}), f32[32,1,1,8]{3,2,1,0:T(1,128)S(1)}, u32[]{:S(2)}, u32[]{:S(2)}) async-start(f32[32,1,1,8]{3,2,1,0:T(1,128)} %bitcast.13), calls=%async_computation.1 | async-start | bytes 32768 | tf_op jit(solution)/shard_map/all_to_all | solution.py:69
  62.5 1.4 gather_fusion.1
  63.9 0.0 copy-done.2
  63.9 0.3 fusion.15
  64.2 0.1 exponential_multiply_fusion.1
  64.3 0.7 fusion.27
  65.1 3.8 %fusion.10 = f32[96,8,128]{2,1,0:T(8,128)S(1)} fusion(bf16[96,1,256,128]{3,2,1,0:T(8,128)(2,1)} %param.12, f32[96,8,256]{2,1,0:T(8,128)S(1)} %get-tuple-element.14, f32[96,256]{1,0:T(8,128)S(1)} %get-tuple-element.9, f32[96,8]{1,0:T(8,128)S(1)} %get-tuple-element.13, f32[96,8]{1,0:T(8,128)S(1)} %exponential_multiply_fusion.1), kind=kOutput, calls=%fused_computation.8 | convolution fusion | flops 51019776 | bytes 7575552 | tf_op jit(solution)/shard_map/skgb,skbd->skgd/dot_general | solution.py:35
  68.9 0.0 copy-done.3
  68.9 0.3 convolution_bitcast_fusion.1
  69.2 0.7 copy.22
  69.9 1.1 all-to-all-done.1
  71.0 8.2 %all-to-all-start.2 = ((f32[32,1,1,8]{3,2,1,0:T(1,128)}), f32[32,1,1,8]{3,2,1,0:T(1,128)S(1)}, u32[]{:S(2)}, u32[]{:S(2)}) async-start(f32[32,1,1,8]{3,2,1,0:T(1,128)} %bitcast.34), calls=%async_computation.2 | async-start | bytes 32768 | tf_op jit(solution)/shard_map/all_to_all | solution.py:70
  79.1 0.1 reduce_max.32
  79.2 0.0 copy-done.1
  79.2 0.0 copy-done.4
  79.2 0.1 fusion.40
  79.3 8.4 %all-to-all-done.2 = f32[32,1,1,8]{3,2,1,0:T(1,128)S(1)} async-done(((f32[32,1,1,8]{3,2,1,0:T(1,128)}), f32[32,1,1,8]{3,2,1,0:T(1,128)S(1)}, u32[]{:S(2)}, u32[]{:S(2)}) %all-to-all-start.2) | async-done | bytes 1056 | tf_op jit(solution)/shard_map/all_to_all | solution.py:70
  87.7 3.9 %all-to-all-start = ((f32[32,1,1,8,128]{4,3,2,1,0:T(8,128)}), f32[32,1,1,8,128]{4,3,2,1,0:T(8,128)S(1)}, u32[]{:S(2)}, u32[]{:S(2)}) async-start(f32[32,1,1,8,128]{4,3,2,1,0:T(8,128)} %copy.22), calls=%async_computation | async-start | bytes 262144 | tf_op jit(solution)/shard_map/all_to_all | solution.py:71
  91.6 0.0 reduce-scatter.4.cloned.1.call-start
  91.7 9.3 %all-to-all-done = f32[32,1,1,8,128]{4,3,2,1,0:T(8,128)S(1)} async-done(((f32[32,1,1,8,128]{4,3,2,1,0:T(8,128)}), f32[32,1,1,8,128]{4,3,2,1,0:T(8,128)S(1)}, u32[]{:S(2)}, u32[]{:S(2)}) %all-to-all-start) | async-done | bytes 131104 | tf_op jit(solution)/shard_map/all_to_all | solution.py:71
  101.0 0.1 fusion.21
  101.1 0.1 div.20
  101.2 0.1 mul.124
  101.3 32.2 %all-gather = bf16[32,1,1024]{2,1,0:T(2,128)(2,1)S(1)} all-gather(bf16[1,1,1024]{2,1,0:T(2,128)(2,1)S(1)} %convert_bitcast_fusion), channel_id=1, replica_groups=mesh['grp'=32,'tp'=8] {'grp'}, dimensions={0}, use_global_device_ids=true | all-gather | bytes 67584 | tf_op jit(solution)/shard_map/all_gather | solution.py:82
  133.5 0.0 copy-done
  133.5 1.0 convolution_bitcast_fusion
  134.5 0.0 reduce-scatter.4.cloned.1.call-update
  134.5 51.5 %reduce-scatter.4.cloned.1.call-done = f32[32,32]{1,0:T(8,128)} async-done(((f32[256,32]{1,0:T(8,128)}), f32[32,32]{1,0:T(8,128)}) %reduce-scatter.4.cloned.1.call-update) | async-done | bytes 4112
  186.1 1.4 copy.26
  (10 shorter events, 0.1 us)
Async XLA Ops:
  6.5 127.0 %copy-start = (bf16[1024,256]{1,0:T(8,128)(2,1)S(1)}, bf16[1024,256]{1,0:T(8,128)(2,1)}, u32[]{:S(2)}) copy-start(bf16[1024,256]{1,0:T(8,128)(2,1)} %param.15) | copy-start | bytes 1572868
  6.5 57.4 %copy-start.2 = (s32[96,2]{0,1:T(2,128)S(1)}, s32[96,2]{0,1:T(2,128)}, u32[]{:S(2)}) copy-start(s32[96,2]{0,1:T(2,128)} %param.14) | copy-start | bytes 2308
  55.9 13.0 %copy-start.3 = (bf16[1,1,128]{2,1,0:T(2,128)(2,1)S(1)}, bf16[1,1,128]{2,1,0:T(2,128)(2,1)}, u32[]{:S(2)}) copy-start(bf16[1,1,128]{2,1,0:T(2,128)(2,1)} %param.10) | copy-start | bytes 772
  55.9 23.3 %copy-start.1 = (bf16[1,8,128]{2,1,0:T(8,128)(2,1)S(1)}, bf16[1,8,128]{2,1,0:T(8,128)(2,1)}, u32[]{:S(2)}) copy-start(bf16[1,8,128]{2,1,0:T(8,128)(2,1)} %param.8) | copy-start | bytes 6148
  55.9 23.3 %copy-start.4 = (bf16[1,1,128]{2,1,0:T(2,128)(2,1)S(1)}, bf16[1,1,128]{2,1,0:T(2,128)(2,1)}, u32[]{:S(2)}) copy-start(bf16[1,1,128]{2,1,0:T(2,128)(2,1)} %param.9) | copy-start | bytes 772
  56.7 14.3 %all-to-all-start.1 = ((f32[32,1,1,8]{3,2,1,0:T(1,128)}), f32[32,1,1,8]{3,2,1,0:T(1,128)S(1)}, u32[]{:S(2)}, u32[]{:S(2)}) async-start(f32[32,1,1,8]{3,2,1,0:T(1,128)} %bitcast.13), calls=%async_computation.1 | async-start | bytes 32768 | tf_op jit(solution)/shard_map/all_to_all | solution.py:69
  71.0 16.8 %all-to-all-start.2 = ((f32[32,1,1,8]{3,2,1,0:T(1,128)}), f32[32,1,1,8]{3,2,1,0:T(1,128)S(1)}, u32[]{:S(2)}, u32[]{:S(2)}) async-start(f32[32,1,1,8]{3,2,1,0:T(1,128)} %bitcast.34), calls=%async_computation.2 | async-start | bytes 32768 | tf_op jit(solution)/shard_map/all_to_all | solution.py:70
  87.7 13.3 %all-to-all-start = ((f32[32,1,1,8,128]{4,3,2,1,0:T(8,128)}), f32[32,1,1,8,128]{4,3,2,1,0:T(8,128)S(1)}, u32[]{:S(2)}, u32[]{:S(2)}) async-start(f32[32,1,1,8,128]{4,3,2,1,0:T(8,128)} %copy.22), calls=%async_computation | async-start | bytes 262144 | tf_op jit(solution)/shard_map/all_to_all | solution.py:71
  91.6 94.5 %reduce-scatter.4.cloned.1.call-start = ((), (), s32[]{:S(2)}) async-start(), calls=%async_computation.4 | async-start | bytes 147456
Sparse Core Ops, SparseCore 0:
  134.6 51.3 reduce-scatter.3
where the time goes:
time: 196 us; the launch traced here: 194 us
  blocking collectives  72.8 us (37%)
  waiting for transfers between devices  70.3 us (36%)
  starting transfers between devices  17.9 us (9%)
  between operations  13.5 us (7%)
  matrix products  10.8 us (6%)
  local copies, waits for them, and re-layouts  5.3 us (3%)
  other arithmetic  3.67 us (2%)
    unnamed x2, waiting for transfers between devices  51.6 us
    all_gather x1, blocking collectives, body(): q_all = lax.all_gather(queries, 'grp', axis=0, tiled=True)  40.5 us
    all_gather x1, blocking collectives, body(): lax.all_gather(attention, 'grp', axis=0, tiled=True)  32.2 us
    all_to_all x1, waiting for transfers between devices, body(): lax.all_to_all(value_sum[:, None], 'grp', split_axis=0, concat_axis=1, ti...  9.3 us
    all_to_all x1, waiting for transfers between devices, body(): lax.all_to_all(weight_sum[:, None], 'grp', split_axis=0, concat_axis=1, t...  8.41 us
    all_to_all x1, starting transfers between devices, body(): lax.all_to_all(weight_sum[:, None], 'grp', split_axis=0, concat_axis=1, t...  8.15 us
    all_to_all x1, starting transfers between devices, body(): lax.all_to_all(best[:, None], 'grp', split_axis=0, concat_axis=1, tiled=T...  5.86 us
    dot_general x1, matrix products, slot_terms(): jnp.einsum('skgd,skbd->skgb', picked, keys, preferred_element_type=jnp.fl...  4.59 us
  transfers between devices with their start and end apart: 4, of which 4 were waited for; matrix products, arithmetic and copies ran while one was open for 4% of the time, Pallas kernels for 0%

commit v1 on v0

v1 whole, which is shorter than its diff:
```python
import functools
import math

import jax
import jax.numpy as jnp
from jax import lax
from jax.experimental import pallas as pl
from jax.experimental.pallas import tpu as pltpu
from jax.sharding import PartitionSpec as P

MESH = pl.DeviceIdType.MESH
NEG = -1e30
F32 = jnp.float32
BF16 = jnp.bfloat16


def hops(offset, z_extent, y_extent):
    z, y = offset // y_extent, offset % y_extent
    return min(z, z_extent - z) + min(y, y_extent - y)


def kernel(
    grp_count,
    tp_count,
    q_hbm,
    nk_hbm,
    nv_hbm,
    k_hbm,
    v_hbm,
    len_ref,
    place_ref,
    w_hbm,
    out_ref,
    q_all,
    nk,
    nv,
    keys,
    vals,
    w,
    q_sel,
    scores,
    group_max,
    mix,
    tot,
    msg_f,
    msg,
    got,
    att,
    att_f,
    part_out,
    part_in,
    sem_small,
    sem_k,
    sem_v,
    sem_w,
    send_sems,
    recv_sems,
):
    g = lax.axis_index("grp")
    t = lax.axis_index("tp")
    slots, tokens, head = keys.shape
    heads = q_all.shape[1]
    scale = head**-0.5 * math.log2(math.e)

    order = sorted(range(1, grp_count), key=lambda i: -hops(i, grp_count // 4, 4))
    tp_order = sorted(range(1, tp_count), key=lambda i: -min(i, tp_count - i))

    def grp_peer(i):
        return lax.rem(g + i, grp_count)

    def tp_peer(i):
        return lax.rem(t + i, tp_count)

    barrier = pltpu.get_barrier_semaphore()
    for i in order:
        pl.semaphore_signal(barrier, 1, device_id={"grp": grp_peer(i)}, device_id_type=MESH)
    for i in tp_order:
        pl.semaphore_signal(barrier, 1, device_id={"tp": tp_peer(i)}, device_id_type=MESH)

    small = [
        pltpu.make_async_copy(q_hbm.at[0], q_all.at[g], sem_small.at[0]),
        pltpu.make_async_copy(nk_hbm.at[0], nk, sem_small.at[1]),
        pltpu.make_async_copy(nv_hbm.at[0], nv, sem_small.at[2]),
    ]
    for c in small:
        c.start()
    big = [
        pltpu.make_async_copy(k_hbm, keys, sem_k),
        pltpu.make_async_copy(v_hbm, vals, sem_v),
        pltpu.make_async_copy(w_hbm, w, sem_w),
    ]
    for c in big:
        c.start()
    for c in small:
        c.wait()

    lane = lax.broadcasted_iota(jnp.int32, (heads, 128), 1)
    row = lax.broadcasted_iota(jnp.int32, (grp_count, 128), 0)
    token = lax.broadcasted_iota(jnp.int32, (heads, tokens), 1)

    owner_row = jnp.full((heads, 128), grp_count, jnp.int32)
    for s in range(slots):
        owner_row = jnp.where(lane == s, place_ref[s, 0], owner_row)
    onehot = jnp.where(owner_row[:1, :] == row, 1.0, 0.0)[:, :slots].astype(BF16)
    onehot2 = jnp.concatenate([onehot, onehot], axis=1)

    pl.semaphore_wait(barrier, grp_count - 1 + tp_count - 1)
    for i in order:
        pltpu.make_async_remote_copy(
            q_all.at[g],
            q_all.at[g],
            send_sems.at[0],
            recv_sems.at[0],
            device_id={"grp": grp_peer(i)},
            device_id_type=MESH,
        ).start()
    big[0].wait()
    others = q_all.at[pl.ds(0, grp_count - 1)]
    pltpu.make_async_copy(others, others, recv_sems.at[0]).wait()

    chunk = 24
    for c in range(slots // chunk):
        for s in range(c * chunk, (c + 1) * chunk):
            q_sel[s] = q_all[jnp.minimum(place_ref[s, 0], grp_count - 1)]
    slot_max = jnp.full((heads, 128), NEG, F32)
    for s in range(slots):
        owner = place_ref[s, 0]
        live = len_ref[jnp.minimum(owner, grp_count - 1)] - place_ref[s, 1] * tokens
        live = jnp.where(owner < grp_count, live, 0)
        x = lax.dot_general(
            q_sel[s], keys[s], (((1,), (1,)), ((), ())), preferred_element_type=F32
        )
        x = jnp.where(token < live, x * scale, NEG)
        scores[s] = x
        slot_max = jnp.where(lane == s, jnp.max(x, axis=1, keepdims=True), slot_max)
    for r in range(grp_count):
        top = jnp.max(jnp.where(owner_row == r, slot_max, NEG), axis=1, keepdims=True)
        group_max[r] = jnp.broadcast_to(top, (heads, 128))

    ones = jnp.ones((tokens, 128), BF16)
    big[1].wait()
    for s in range(slots):
        top = group_max[jnp.minimum(place_ref[s, 0], grp_count - 1)]
        p = jnp.exp2(scores[s] - jnp.concatenate([top, top], axis=1)).astype(BF16)
        mix[s] = jnp.dot(p, vals[s], preferred_element_type=F32)
        tot[s] = jnp.dot(p, ones, preferred_element_type=F32)

    lane_r = lax.broadcasted_iota(jnp.int32, (grp_count, 128), 1)
    for h in range(heads):
        both = jnp.concatenate([mix[:, h, :], tot[:, h, :]], axis=1)
        hi = both.astype(BF16)
        lo = (both - hi.astype(F32)).astype(BF16)
        sums = jnp.dot(onehot2, jnp.concatenate([hi, lo], axis=0), preferred_element_type=F32)
        value_sum, weight_sum = sums[:, :128], sums[:, 128:]
        there = weight_sum > 0.0
        safe = jnp.where(there, weight_sum, 1.0)
        norm = value_sum / safe
        lse = jnp.where(there, group_max[:, h, :] + jnp.log2(safe), NEG)
        first = lse.astype(BF16).astype(F32)
        rest = lse - first
        second = rest.astype(BF16).astype(F32)
        third = rest - second
        stat = jnp.where(lane_r == g, first, 0.0)
        stat = jnp.where(lane_r == g + 32, second, stat)
        stat = jnp.where(lane_r == g + 64, third, stat)
        msg_f[:, h, :] = norm
        msg_f[:, heads + h, :] = stat
    for r in range(grp_count):
        msg[r] = msg_f[r].astype(BF16)
    got[g] = msg[g]
    for i in order:
        pltpu.make_async_remote_copy(
            msg.at[grp_peer(i)],
            got.at[g],
            send_sems.at[1],
            recv_sems.at[1],
            device_id={"grp": grp_peer(i)},
            device_id_type=MESH,
        ).start()

    new_score = scale * jnp.sum(
        q_all[g].astype(F32) * nk[...].astype(F32), axis=1, keepdims=True
    )
    others = got.at[pl.ds(0, grp_count - 1)]
    pltpu.make_async_copy(others, others, recv_sems.at[1]).wait()

    stat = got[0, heads:, :].astype(F32)
    for r in range(1, grp_count):
        stat = stat + got[r, heads:, :].astype(F32)
    lse = stat + pltpu.roll(stat, 96, 1) + pltpu.roll(stat, 64, 1)
    lse = jnp.where(lane < grp_count, lse, NEG)
    top = jnp.maximum(jnp.max(lse, axis=1, keepdims=True), new_score)
    share = jnp.exp2(lse - top)
    own = jnp.exp2(new_score - top)
    total = jnp.sum(share, axis=1, keepdims=True) + own
    summed = own * nv[...].astype(F32)
    for r in range(grp_count):
        summed = summed + share[:, r : r + 1] * got[r, :heads, :].astype(F32)
    att[g] = (summed / total).astype(BF16)

    for i in order:
        pltpu.make_async_remote_copy(
            att.at[g],
            att.at[g],
            send_sems.at[2],
            recv_sems.at[2],
            device_id={"grp": grp_peer(i)},
            device_id_type=MESH,
        ).start()
    big[2].wait()
    others = att.at[pl.ds(0, grp_count - 1)]
    pltpu.make_async_copy(others, others, recv_sems.at[2]).wait()

    for r in range(grp_count):
        att_f[r] = att[r].astype(F32)
    flat = jnp.concatenate([att_f[:, h, :] for h in range(heads)], axis=1).astype(BF16)
    part = jnp.dot(flat, w[...], preferred_element_type=F32)

    rows = grp_count // 8
    width = part.shape[1] // tp_count
    for p in range(tp_count):
        at = p * width
        tile = jnp.zeros((8, 128), F32)
        for j in range(rows):
            piece = part[8 * j : 8 * j + 8, at // 128 * 128 : at // 128 * 128 + 128]
            shift = (width * j - at) % 128
            if shift:
                piece = pltpu.roll(piece, shift, 1)
            tile = jnp.where(lane // width == j, piece, tile)
        part_out[p] = tile
    part_in[t] = part_out[t]
    for i in tp_order:
        pltpu.make_async_remote_copy(
            part_out.at[tp_peer(i)],
            part_in.at[t],
            send_sems.at[3],
            recv_sems.at[3],
            device_id={"tp": tp_peer(i)},
            device_id_type=MESH,
        ).start()
    others = part_in.at[pl.ds(0, tp_count - 1)]
    pltpu.make_async_copy(others, others, recv_sems.at[3]).wait()
    tile = part_in[0]
    for p in range(1, tp_count):
        tile = tile + part_in[p]
    out_ref[...] = jnp.concatenate(
        [tile[:, width * j : width * (j + 1)] for j in range(rows)], axis=0
    ).astype(BF16)

    for k, ref in enumerate((q_all, got, att)):
        others = ref.at[pl.ds(0, grp_count - 1)]
        pltpu.make_async_copy(others, others, send_sems.at[k]).wait()
    others = part_out.at[pl.ds(0, tp_count - 1)]
    pltpu.make_async_copy(others, others, send_sems.at[3]).wait()


def body(
    queries, new_keys, new_values, key_cache, paged_value_cache, lengths, placement, out_weight
):
    grp_count, tp_count = lax.axis_size("grp"), lax.axis_size("tp")
    slots, _, tokens, head = key_cache.shape
    heads = queries.shape[1]
    requests = lengths.shape[0]
    any_space = pl.BlockSpec(memory_space=pl.ANY)
    scalars = pl.BlockSpec(memory_space=pltpu.SMEM)
    return pl.pallas_call(
        functools.partial(kernel, grp_count, tp_count),
        out_shape=jax.ShapeDtypeStruct((requests, out_weight.shape[1] // tp_count), BF16),
        in_specs=[any_space] * 5 + [scalars] * 2 + [any_space],
        out_specs=pl.BlockSpec(memory_space=pltpu.VMEM),
        scratch_shapes=[
            pltpu.VMEM((requests, heads, head), BF16),
            pltpu.VMEM((1, head), BF16),
            pltpu.VMEM((1, head), BF16),
            pltpu.VMEM((slots, tokens, head), BF16),
            pltpu.VMEM((slots, tokens, head), BF16),
            pltpu.VMEM(out_weight.shape, BF16),
            pltpu.VMEM((slots, heads, head), BF16),
            pltpu.VMEM((slots, heads, tokens), F32),
            pltpu.VMEM((requests, heads, head), F32),
            pltpu.VMEM((slots, heads, head), F32),
            pltpu.VMEM((slots, heads, head), F32),
            pltpu.VMEM((requests, 2 * heads, head), F32),
            pltpu.VMEM((requests, 2 * heads, head), BF16),
            pltpu.VMEM((requests, 2 * heads, head), BF16),
            pltpu.VMEM((requests, heads, head), BF16),
            pltpu.VMEM((requests, heads, head), F32),
            pltpu.VMEM((tp_count, 8, 128), F32),
            pltpu.VMEM((tp_count, 8, 128), F32),
            pltpu.SemaphoreType.DMA((3,)),
            pltpu.SemaphoreType.DMA,
            pltpu.SemaphoreType.DMA,
            pltpu.SemaphoreType.DMA,
            pltpu.SemaphoreType.DMA((4,)),
            pltpu.SemaphoreType.DMA((4,)),
        ],
        compiler_params=pltpu.CompilerParams(
            collective_id=0, has_side_effects=True, vmem_limit_bytes=48 << 20
        ),
    )(
        queries,
        new_keys,
        new_values,
        key_cache.reshape(slots, tokens, head),
        paged_value_cache.reshape(slots, tokens, head),
        lengths,
        placement,
        out_weight,
    )


def solution(mesh):
    in_specs = (
        P("grp", "tp", None),
        P("grp", "tp", None),
        P("grp", "tp", None),
        P("grp", "tp", None, None),
        P("grp", "tp", None, None),
        P(),
        P("grp", None),
        P("tp", "grp"),
    )
    out_specs = P(None, ("grp", "tp"))
    return jax.shard_map(body, mesh=mesh, in_specs=in_specs, out_specs=out_specs, check_vma=False)
```

time: 196 us -> 44 us (0.22)
  blocking collectives: 72.8 us -> 0 us
  waiting for transfers between devices: 70.3 us -> 0 us
  Pallas kernels: 0 us -> 38.7 us
  starting transfers between devices: 17.9 us -> 0 us
  between operations: 13.5 us -> 0.02 us
  matrix products: 10.8 us -> 0 us
  other arithmetic: 3.67 us -> 0 us
    all_gather x2 -> x0, blocking collectives: 72.8 us -> none  [the longest x1 40.5 us: body(): q_all = lax.all_gather(queries, 'grp', axis=0, tiled=True)]
    unnamed x2 -> x0, waiting for transfers between devices: 51.6 us -> none
    pallas_call x0 -> x1, Pallas kernels: none -> 38.7 us  [body(): pl.pallas_call(functools.partial(kernel, grp_count, tp_count), out_shape=...]
    all_to_all x3 -> x0, waiting for transfers between devices: 18.8 us -> none  [the longest x1 9.3 us: body(): lax.all_to_all(value_sum[:, None], 'grp', split_axis=0, concat_axis=1, ti...]
    all_to_all x3 -> x0, starting transfers between devices: 17.9 us -> none  [the longest x1 8.15 us: body(): lax.all_to_all(weight_sum[:, None], 'grp', split_axis=0, concat_axis=1, t...]
    dot_general x6 -> x0, matrix products: 9.79 us -> none  [the longest x1 4.59 us: slot_terms(): jnp.einsum('skgd,skbd->skgb', picked, keys, preferred_element_type=jnp.fl...]
    unnamed x12, local copies, waits for them, and re-layouts: 1.44 us -> 5.06 us
    gather x2 -> x0, local copies, waits for them, and re-layouts: 2.95 us -> none  [the longest x1 1.59 us: slot_terms(): live_len = jnp.take(lengths, clamped)]
  transfers between devices with their start and end apart: 4 -> 0, of which waited for: 4 -> 0; matrix products, arithmetic and copies ran while one was open for 4% -> 0% of each run, Pallas kernels for 0% -> 0%
where the time goes in v1:
time: 44 us; the launch traced here: 43.8 us
  Pallas kernels  38.7 us (88%)
  local copies, waits for them, and re-layouts  5.06 us (11%)
    pallas_call x1, Pallas kernels, body(): pl.pallas_call(functools.partial(kernel, grp_count, tp_count), out_shape=...  38.7 us
    unnamed x12, local copies, waits for them, and re-layouts  5.06 us

profile of v1, /device:TPU:1, one launch (start us, length us, event | category | flops | bytes accessed | tf_op | source)
XLA Modules:
  0.0 43.8 jit_solution(6219268383575751449)
XLA Ops:
  0.0 0.8 %copy.9.place_ref = s32[96,2]{1,0:T(8,128)S(1)} copy(s32[96,2]{0,1:T(2,128)} %param.14) | data formatting | bytes 1536 | tf_op args[6]
  0.8 0.0 copy-start
  0.8 1.0 %copy-done = bf16[1024,256]{1,0:T(8,128)(2,1)S(1)} copy-done((bf16[1024,256]{1,0:T(8,128)(2,1)S(1)}, bf16[1024,256]{1,0:T(8,128)(2,1)}, u32[]{:S(2)}) %copy-start) | copy-done | bytes 524312
  1.8 0.0 copy-start.1
  1.8 0.7 %copy-done.1 = bf16[1,8,128]{2,1,0:T(8,128)(2,1)S(1)} copy-done((bf16[1,8,128]{2,1,0:T(8,128)(2,1)S(1)}, bf16[1,8,128]{2,1,0:T(8,128)(2,1)}, u32[]{:S(2)}) %copy-start.1) | copy-done | bytes 2072
  2.5 0.0 copy-start.2
  2.5 0.7 %copy-done.2 = bf16[1,1,128]{2,1,0:T(2,128)(2,1)S(1)} copy-done((bf16[1,1,128]{2,1,0:T(2,128)(2,1)S(1)}, bf16[1,1,128]{2,1,0:T(2,128)(2,1)}, u32[]{:S(2)}) %copy-start.2) | copy-done | bytes 280
  3.2 0.0 copy-start.3
  3.2 0.7 %copy-done.3 = bf16[1,1,128]{2,1,0:T(2,128)(2,1)S(1)} copy-done((bf16[1,1,128]{2,1,0:T(2,128)(2,1)S(1)}, bf16[1,1,128]{2,1,0:T(2,128)(2,1)}, u32[]{:S(2)}) %copy-start.3) | copy-done | bytes 280
  3.8 0.0 copy-start.4
  3.8 0.7 %copy-done.4 = s32[32]{0:T(128)S(1)} copy-done((s32[32]{0:T(128)S(1)}, s32[32]{0:T(128)}, u32[]{:S(2)}) %copy-start.4) | copy-done | bytes 152
  4.5 38.7 %shard_map.82 = bf16[32,32]{1,0:T(8,128)(2,1)S(1)} custom-call(bf16[1,8,128]{2,1,0:T(8,128)(2,1)S(1)} %copy-done.1, bf16[1,1,128]{2,1,0:T(2,128)(2,1)S(1)} %copy-done.2, bf16[1,1,128]{2,1,0:T(2,128)(2,1)S(1)} %copy-done.3, bf16[96,256,128]{2,1,0:T(8,128)(2,1)} %bitcast.2, bf16[96,256,128]{2,1,0:T(8,128)(2,1)} %bitcast.3, s32[32]{0:T(128)S(1)} %copy-done.4, ...), custom_call_target="tpu_custom_call" | custom-call | tf_op jit(solution)/shard_map/pallas_call | solution.py:266
  43.2 0.6 %copy.11 = bf16[32,32]{1,0:T(8,128)(2,1)} copy(bf16[32,32]{1,0:T(8,128)(2,1)S(1)} %shard_map.82) | data formatting | bytes 4096
Async XLA Ops:
  0.8 1.0 %copy-start = (bf16[1024,256]{1,0:T(8,128)(2,1)S(1)}, bf16[1024,256]{1,0:T(8,128)(2,1)}, u32[]{:S(2)}) copy-start(bf16[1024,256]{1,0:T(8,128)(2,1)} %w_hbm.1) | copy-start | bytes 1572868
  1.8 0.7 %copy-start.1 = (bf16[1,8,128]{2,1,0:T(8,128)(2,1)S(1)}, bf16[1,8,128]{2,1,0:T(8,128)(2,1)}, u32[]{:S(2)}) copy-start(bf16[1,8,128]{2,1,0:T(8,128)(2,1)} %q_hbm.1) | copy-start | bytes 6148
  2.5 0.7 %copy-start.2 = (bf16[1,1,128]{2,1,0:T(2,128)(2,1)S(1)}, bf16[1,1,128]{2,1,0:T(2,128)(2,1)}, u32[]{:S(2)}) copy-start(bf16[1,1,128]{2,1,0:T(2,128)(2,1)} %nk_hbm.1) | copy-start | bytes 772
  3.2 0.7 %copy-start.3 = (bf16[1,1,128]{2,1,0:T(2,128)(2,1)S(1)}, bf16[1,1,128]{2,1,0:T(2,128)(2,1)}, u32[]{:S(2)}) copy-start(bf16[1,1,128]{2,1,0:T(2,128)(2,1)} %nv_hbm.1) | copy-start | bytes 772
  3.8 0.7 %copy-start.4 = (s32[32]{0:T(128)S(1)}, s32[32]{0:T(128)}, u32[]{:S(2)}) copy-start(s32[32]{0:T(128)} %len_ref.1) | copy-start | bytes 388

commit v2 on v1

v2 whole, which is shorter than its diff:
```python
import functools
import math

import jax
import jax.numpy as jnp
from jax import lax
from jax.experimental import pallas as pl
from jax.experimental.pallas import tpu as pltpu
from jax.sharding import PartitionSpec as P

MESH = pl.DeviceIdType.MESH
NEG = -1e30
F32 = jnp.float32
BF16 = jnp.bfloat16


def torus(z_extent, y_extent):
    found = []
    for dz in range(z_extent):
        for dy in range(y_extent):
            far = min(dz, z_extent - dz) + min(dy, y_extent - dy)
            if far:
                found.append((far, dz, dy))
    return sorted(found, key=lambda f: (-f[0], f[1], f[2]))


def tree(terms):
    while len(terms) > 1:
        terms = [a + b for a, b in zip(terms[::2], terms[1::2])] + terms[len(terms) // 2 * 2 :]
    return terms[0]


Z, Y = 8, 4
OFFSETS = torus(Z, Y)
NEAR = [f for f in OFFSETS if f[0] < 3 or f in ((3, 1, 2), (3, 7, 2), (3, 2, 1), (3, 6, 1))]
NEAR = sorted(NEAR, key=lambda f: -f[0])


def kernel(
    grp_count,
    tp_count,
    q_hbm,
    nk_hbm,
    nv_hbm,
    k_hbm,
    v_hbm,
    len_hbm,
    place_hbm,
    w_hbm,
    out_ref,
    q_all,
    nk,
    nv,
    keys,
    keys_t,
    vals,
    w,
    len_ref,
    place_ref,
    scores,
    group_max,
    mix,
    tot,
    norm_f,
    msg,
    got,
    stat_out,
    stat_in,
    att,
    att_f,
    part_out,
    part_in,
    sem_small,
    sem_k,
    sem_v,
    sem_w,
    send_sems,
    recv_sems,
):
    g = lax.axis_index("grp")
    t = lax.axis_index("tp")
    slots, tokens, head = keys.shape
    heads = q_all.shape[1]
    padded = mix.shape[0]
    scale = head**-0.5 * math.log2(math.e)
    gz, gy = g // Y, lax.rem(g, Y)
    tp_order = sorted(range(1, tp_count), key=lambda i: -min(i, tp_count - i))

    def grp_at(dz, dy):
        return lax.rem(gz + dz, Z) * Y + lax.rem(gy + dy, Y)

    def tp_peer(i):
        return lax.rem(t + i, tp_count)

    def push(src, dst, k, device_id):
        pltpu.make_async_remote_copy(
            src,
            dst,
            send_sems.at[k],
            recv_sems.at[k],
            device_id=device_id,
            device_id_type=MESH,
        ).start()

    def await_bytes(ref, count, sem):
        some = ref.at[pl.ds(0, count)]
        pltpu.make_async_copy(some, some, sem).wait()

    barrier = pltpu.get_barrier_semaphore()
    for _, dz, dy in OFFSETS:
        pl.semaphore_signal(barrier, 1, device_id={"grp": grp_at(dz, dy)}, device_id_type=MESH)
    for i in tp_order:
        pl.semaphore_signal(barrier, 1, device_id={"tp": tp_peer(i)}, device_id_type=MESH)

    small = [
        pltpu.make_async_copy(q_hbm.at[0], q_all.at[g], sem_small.at[0]),
        pltpu.make_async_copy(nk_hbm.at[0], nk, sem_small.at[1]),
        pltpu.make_async_copy(nv_hbm.at[0], nv, sem_small.at[2]),
        pltpu.make_async_copy(len_hbm, len_ref, sem_small.at[3]),
        pltpu.make_async_copy(place_hbm, place_ref, sem_small.at[4]),
    ]
    for c in small:
        c.start()
    big = [
        pltpu.make_async_copy(k_hbm, keys, sem_k),
        pltpu.make_async_copy(v_hbm, vals, sem_v),
        pltpu.make_async_copy(w_hbm, w, sem_w),
    ]
    for c in big:
        c.start()
    for c in small:
        c.wait()

    pl.semaphore_wait(barrier, grp_count - 1 + tp_count - 1)
    for _, dz, dy in OFFSETS:
        push(q_all.at[g], q_all.at[g], 0, {"grp": grp_at(dz, dy)})

    lane = lax.broadcasted_iota(jnp.int32, (heads, 128), 1)
    row = lax.broadcasted_iota(jnp.int32, (grp_count, 128), 0)
    lane_r = lax.broadcasted_iota(jnp.int32, (grp_count, 128), 1)
    token = lax.broadcasted_iota(jnp.int32, (heads, tokens), 1)

    owner_row = jnp.where(lane == slots, g, grp_count)
    for s in range(slots):
        owner_row = jnp.where(lane == s, place_ref[0, s], owner_row)
    onehot = jnp.where(owner_row[:1, :] == row, 1.0, 0.0)[:, :padded].astype(BF16)
    onehot2 = jnp.concatenate([onehot, onehot], axis=1)
    for s in range(slots, padded):
        mix[s] = jnp.zeros((heads, head), F32)
        tot[s] = jnp.zeros((heads, head), F32)
    new_score = scale * jnp.sum(
        q_all[g].astype(F32) * nk[...].astype(F32), axis=1, keepdims=True
    )
    new_score = jnp.broadcast_to(new_score, (heads, 128))
    big[0].wait()
    for s in range(slots):
        keys_t[s] = keys[s].T
    await_bytes(q_all, grp_count - 1, recv_sems.at[0])

    slot_max = jnp.where(lane == slots, new_score, NEG)
    for s in range(slots):
        owner = place_ref[0, s]
        request = jnp.minimum(owner, grp_count - 1)
        live = jnp.where(owner < grp_count, len_ref[request] - place_ref[1, s] * tokens, 0)
        x = jnp.dot(q_all[request], keys_t[s], preferred_element_type=F32)
        x = jnp.where(token < live, x * scale, NEG)
        scores[s] = x
        slot_max = jnp.where(lane == s, jnp.max(x, axis=1, keepdims=True), slot_max)
    for r in range(grp_count):
        top = jnp.max(jnp.where(owner_row == r, slot_max, NEG), axis=1, keepdims=True)
        group_max[r] = jnp.broadcast_to(top, (heads, 128))

    weight = jnp.exp2(new_score - group_max[g])
    mix[slots] = weight * nv[...].astype(F32)
    tot[slots] = weight
    big[1].wait()
    for s in range(slots):
        top = group_max[jnp.minimum(place_ref[0, s], grp_count - 1)]
        p = jnp.exp2(scores[s] - jnp.concatenate([top, top], axis=1))
        mix[s] = jnp.dot(p.astype(BF16), vals[s], preferred_element_type=F32)
        tot[s] = jnp.broadcast_to(jnp.sum(p, axis=1, keepdims=True), (heads, head))

    stat = jnp.full((grp_count, 128), NEG, F32)
    for h in range(heads):
        both = jnp.concatenate([mix[:, h, :], tot[:, h, :]], axis=1)
        hi = both.astype(BF16)
        lo = (both - hi.astype(F32)).astype(BF16)
        sums = jnp.dot(onehot2, jnp.concatenate([hi, lo], axis=0), preferred_element_type=F32)
        value_sum, weight_sum = sums[:, :128], sums[:, 128:]
        there = weight_sum > 0.0
        safe = jnp.where(there, weight_sum, 1.0)
        norm_f[:, h, :] = value_sum / safe
        lse = jnp.where(there, group_max[:, h, :] + jnp.log2(safe), NEG)
        stat = jnp.where(lane_r == h, lse, stat)
    other = jnp.concatenate([stat[grp_count // 2 :], stat[: grp_count // 2]], axis=0)
    other = jnp.where(
        lax.rem(row, 4) < 2, pltpu.roll(other, grp_count - 2, 0), pltpu.roll(other, 2, 0)
    )
    stat = jnp.where((lane_r >= heads) & (lane_r < 2 * heads), pltpu.roll(other, heads, 1), stat)
    stat_out[:, 0, :] = stat
    for r in range(grp_count):
        msg[r] = jnp.concatenate([norm_f[r], norm_f[r ^ 18]], axis=0).astype(BF16)
    got[g] = msg[g]
    stat_in[g] = stat_out[g]
    for _, dz, dy in OFFSETS:
        p = grp_at(dz, dy)
        push(msg.at[p], got.at[g], 1, {"grp": p})
        push(stat_out.at[p], stat_in.at[g], 2, {"grp": p})
    await_bytes(stat_in, grp_count - 1, recv_sems.at[2])
    await_bytes(got, grp_count - 1, recv_sems.at[1])

    lse = stat_in[:, 0, :]
    share = jnp.exp2(lse - jnp.max(lse, axis=0, keepdims=True))
    share = share / jnp.sum(share, axis=0, keepdims=True)
    share = share.T[: 2 * heads, :]
    att[g] = tree(
        [share[:, r : r + 1] * got[r].astype(F32) for r in range(grp_count)]
    ).astype(BF16)

    for _, dz, dy in NEAR:
        push(att.at[g], att.at[g], 3, {"grp": grp_at(dz, dy)})
    big[2].wait()
    await_bytes(att, len(NEAR), recv_sems.at[3])

    for dz, dy in [(0, 0)] + [(dz, dy) for _, dz, dy in NEAR]:
        home = grp_at(Z - dz, Y - dy)
        both = att[home].astype(F32)
        att_f[home] = both[:heads]
        att_f[grp_at(Z - dz + Z // 2, Y - dy + Y // 2)] = both[heads:]
    flat = jnp.concatenate([att_f[:, h, :] for h in range(heads)], axis=1).astype(BF16)
    part = jnp.dot(flat, w[...], preferred_element_type=F32)

    rows = grp_count // 8
    width = part.shape[1] // tp_count
    for p in range(tp_count):
        at = p * width
        tile = jnp.zeros((8, 128), F32)
        for j in range(rows):
            piece = part[8 * j : 8 * j + 8, at // 128 * 128 : at // 128 * 128 + 128]
            shift = (width * j - at) % 128
            if shift:
                piece = pltpu.roll(piece, shift, 1)
            tile = jnp.where(lane // width == j, piece, tile)
        part_out[p] = tile
    part_in[t] = part_out[t]
    for i in tp_order:
        push(part_out.at[tp_peer(i)], part_in.at[t], 4, {"tp": tp_peer(i)})
    await_bytes(part_in, tp_count - 1, recv_sems.at[4])
    tile = tree([part_in[p] for p in range(tp_count)])
    out_ref[...] = jnp.concatenate(
        [tile[:, width * j : width * (j + 1)] for j in range(rows)], axis=0
    ).astype(BF16)

    await_bytes(q_all, grp_count - 1, send_sems.at[0])
    await_bytes(msg, grp_count - 1, send_sems.at[1])
    await_bytes(stat_out, grp_count - 1, send_sems.at[2])
    await_bytes(att, len(NEAR), send_sems.at[3])
    await_bytes(part_out, tp_count - 1, send_sems.at[4])


def body(
    queries, new_keys, new_values, key_cache, paged_value_cache, lengths, placement, out_weight
):
    grp_count, tp_count = lax.axis_size("grp"), lax.axis_size("tp")
    slots, _, tokens, head = key_cache.shape
    heads = queries.shape[1]
    requests = lengths.shape[0]
    padded = slots + 16
    return pl.pallas_call(
        functools.partial(kernel, grp_count, tp_count),
        out_shape=jax.ShapeDtypeStruct((requests, out_weight.shape[1] // tp_count), BF16),
        in_specs=[pl.BlockSpec(memory_space=pltpu.HBM)] * 8,
        out_specs=pl.BlockSpec(memory_space=pltpu.VMEM),
        scratch_shapes=[
            pltpu.VMEM((requests, heads, head), BF16),
            pltpu.VMEM((1, head), BF16),
            pltpu.VMEM((1, head), BF16),
            pltpu.VMEM((slots, tokens, head), BF16),
            pltpu.VMEM((slots, head, tokens), BF16),
            pltpu.VMEM((slots, tokens, head), BF16),
            pltpu.VMEM(out_weight.shape, BF16),
            pltpu.SMEM(lengths.shape, jnp.int32),
            pltpu.SMEM((2, slots), jnp.int32),
            pltpu.VMEM((slots, heads, tokens), F32),
            pltpu.VMEM((requests, heads, head), F32),
            pltpu.VMEM((padded, heads, head), F32),
            pltpu.VMEM((padded, heads, head), F32),
            pltpu.VMEM((requests, heads, head), F32),
            pltpu.VMEM((requests, 2 * heads, head), BF16),
            pltpu.VMEM((requests, 2 * heads, head), BF16),
            pltpu.VMEM((requests, 1, 128), F32),
            pltpu.VMEM((requests, 1, 128), F32),
            pltpu.VMEM((requests, 2 * heads, head), BF16),
            pltpu.VMEM((requests, heads, head), F32),
            pltpu.VMEM((tp_count, 8, 128), F32),
            pltpu.VMEM((tp_count, 8, 128), F32),
            pltpu.SemaphoreType.DMA((5,)),
            pltpu.SemaphoreType.DMA,
            pltpu.SemaphoreType.DMA,
            pltpu.SemaphoreType.DMA,
            pltpu.SemaphoreType.DMA((5,)),
            pltpu.SemaphoreType.DMA((5,)),
        ],
        compiler_params=pltpu.CompilerParams(
            collective_id=0, has_side_effects=True, vmem_limit_bytes=56 << 20
        ),
    )(
        queries,
        new_keys,
        new_values,
        key_cache.reshape(slots, tokens, head),
        paged_value_cache.reshape(slots, tokens, head),
        lengths,
        placement.T,
        out_weight,
    )


def solution(mesh):
    in_specs = (
        P("grp", "tp", None),
        P("grp", "tp", None),
        P("grp", "tp", None),
        P("grp", "tp", None, None),
        P("grp", "tp", None, None),
        P(),
        P("grp", None),
        P("tp", "grp"),
    )
    out_specs = P(None, ("grp", "tp"))
    return jax.shard_map(body, mesh=mesh, in_specs=in_specs, out_specs=out_specs, check_vma=False)
```

time: 44 us -> 36.8 us (0.84)
  local copies, waits for them, and re-layouts: 5.06 us -> 1.3 us
  Pallas kernels: 38.7 us -> 35.3 us
    unnamed x12 -> x1, local copies, waits for them, and re-layouts: 5.06 us -> 1.3 us
    pallas_call x1, Pallas kernels: 38.7 us -> 35.3 us  [body(): pl.pallas_call(functools.partial(kernel, grp_count, tp_count), out_shape=...]
where the time goes in v2:
time: 36.8 us; the launch traced here: 36.6 us
  Pallas kernels  35.3 us (96%)
  local copies, waits for them, and re-layouts  1.3 us (4%)
    pallas_call x1, Pallas kernels, body(): pl.pallas_call(functools.partial(kernel, grp_count, tp_count), out_shape=...  35.3 us
    unnamed x1, local copies, waits for them, and re-layouts  1.3 us

profile of v2, /device:TPU:1, one launch (start us, length us, event | category | flops | bytes accessed | tf_op | source)
XLA Modules:
  0.0 36.6 jit_solution(681385747033959523)
XLA Ops:
  0.0 35.3 %shard_map.82 = bf16[32,32]{1,0:T(8,128)(2,1)} custom-call(bf16[1,8,128]{2,1,0:T(8,128)(2,1)} %q_hbm.1, bf16[1,1,128]{2,1,0:T(2,128)(2,1)} %nk_hbm.1, bf16[1,1,128]{2,1,0:T(2,128)(2,1)} %nv_hbm.1, bf16[96,256,128]{2,1,0:T(8,128)(2,1)} %bitcast.3, bf16[96,256,128]{2,1,0:T(8,128)(2,1)} %bitcast.4, s32[32]{0:T(128)} %len_hbm.1, s32[2,96]{1,0:T(2,128)} %bitcast.5, ...), custom_call_target="tpu_custom_call" | custom-call | tf_op jit(solution)/shard_map/pallas_call | solution.py:269
  35.3 1.3 %copy.10 = bf16[32,32]{1,0:T(8,128)(2,1)} copy(bf16[32,32]{1,0:T(8,128)(2,1)} %shard_map.82) | data formatting | bytes 4096

commit v3 on v2

--- a/solution.py
+++ b/solution.py
@@ -268,7 +268,7 @@
     padded = slots + 16
     return pl.pallas_call(
         functools.partial(kernel, grp_count, tp_count),
-        out_shape=jax.ShapeDtypeStruct((requests, out_weight.shape[1] // tp_count), BF16),
+        out_shape=pltpu.VMEM((requests, out_weight.shape[1] // tp_count), BF16),
         in_specs=[pl.BlockSpec(memory_space=pltpu.HBM)] * 8,
         out_specs=pl.BlockSpec(memory_space=pltpu.VMEM),
         scratch_shapes=[
@@ -302,17 +302,22 @@
             pltpu.SemaphoreType.DMA((5,)),
         ],
         compiler_params=pltpu.CompilerParams(
-            collective_id=0, has_side_effects=True, vmem_limit_bytes=56 << 20
+            collective_id=0, has_side_effects=True, vmem_limit_bytes=32 << 20
         ),
     )(
-        queries,
-        new_keys,
-        new_values,
-        key_cache.reshape(slots, tokens, head),
-        paged_value_cache.reshape(slots, tokens, head),
-        lengths,
-        placement.T,
-        out_weight,
+        *(
+            pltpu.with_memory_space_constraint(x, pltpu.HBM)
+            for x in (
+                queries,
+                new_keys,
+                new_values,
+                key_cache.reshape(slots, tokens, head),
+                paged_value_cache.reshape(slots, tokens, head),
+                lengths,
+                placement.T,
+                out_weight,
+            )
+        )
     )
 
 

time: 36.8 us -> 35.4 us (0.962)
  local copies, waits for them, and re-layouts: 1.3 us -> 0.6 us
  Pallas kernels: 35.3 us -> 34.7 us
    unnamed x1, local copies, waits for them, and re-layouts: 1.3 us -> 0.6 us
    pallas_call x1, Pallas kernels: 35.3 us -> 34.7 us  [body(): pl.pallas_call(functools.partial(kernel, grp_count, tp_count), out_shape=...]
where the time goes in v3:
time: 35.4 us; the launch traced here: 35.3 us
  Pallas kernels  34.7 us (98%)
  local copies, waits for them, and re-layouts  0.6 us (2%)
    pallas_call x1, Pallas kernels, body(): pl.pallas_call(functools.partial(kernel, grp_count, tp_count), out_shape=...  34.7 us

profile of v3, /device:TPU:1, one launch (start us, length us, event | category | flops | bytes accessed | tf_op | source)
XLA Modules:
  0.0 35.3 jit_solution(11400027082959300345)
XLA Ops:
  0.0 34.7 %shard_map.82 = bf16[32,32]{1,0:T(8,128)(2,1)S(1)} custom-call(bf16[1,8,128]{2,1,0:T(8,128)(2,1)} %q_hbm.1, bf16[1,1,128]{2,1,0:T(2,128)(2,1)} %nk_hbm.1, bf16[1,1,128]{2,1,0:T(2,128)(2,1)} %nv_hbm.1, bf16[96,256,128]{2,1,0:T(8,128)(2,1)} %bitcast.3, bf16[96,256,128]{2,1,0:T(8,128)(2,1)} %bitcast.4, s32[32]{0:T(128)} %len_hbm.1, s32[2,96]{1,0:T(2,128)} %bitcast.5, ...), custom_call_target="tpu_custom_call" | custom-call | tf_op jit(solution)/shard_map/pallas_call | solution.py:269
  34.7 0.6 %copy.10 = bf16[32,32]{1,0:T(8,128)(2,1)} copy(bf16[32,32]{1,0:T(8,128)(2,1)S(1)} %shard_map.82) | data formatting | bytes 4096

commit v4 on v3

--- a/solution.py
+++ b/solution.py
@@ -32,7 +32,7 @@
 
 Z, Y = 8, 4
 OFFSETS = torus(Z, Y)
-NEAR = [f for f in OFFSETS if f[0] < 3 or f in ((3, 1, 2), (3, 7, 2), (3, 2, 1), (3, 6, 1))]
+NEAR = [f for f in OFFSETS if f[0] < 3 or f in ((3, 5, 0), (3, 3, 0), (3, 2, 1), (3, 6, 1))]
 NEAR = sorted(NEAR, key=lambda f: -f[0])
 
 
@@ -62,6 +62,7 @@
     mix,
     tot,
     norm_f,
+    adder,
     msg,
     got,
     stat_out,
@@ -143,8 +144,18 @@
     owner_row = jnp.where(lane == slots, g, grp_count)
     for s in range(slots):
         owner_row = jnp.where(lane == s, place_ref[0, s], owner_row)
-    onehot = jnp.where(owner_row[:1, :] == row, 1.0, 0.0)[:, :padded].astype(BF16)
-    onehot2 = jnp.concatenate([onehot, onehot], axis=1)
+    per_tile = 128 // heads
+    big_row = lax.broadcasted_iota(jnp.int32, (grp_count * heads, 128), 0)
+    big_lane = lax.broadcasted_iota(jnp.int32, (grp_count * heads, 128), 1)
+    same_head = lax.rem(big_row, heads) == lax.rem(big_lane, heads)
+    for c in range(padded // per_tile):
+        owners = jnp.full((1, 128), grp_count, jnp.int32)
+        if c * per_tile == slots:
+            owners = jnp.where(lane[:1] < heads, g, grp_count)
+        for s in range(c * per_tile, min(slots, (c + 1) * per_tile)):
+            owners = jnp.where(lane[:1] // heads == s - c * per_tile, place_ref[0, s], owners)
+        block = jnp.where(same_head & (owners == big_row // heads), 1.0, 0.0)
+        adder[:, c * 128 : (c + 1) * 128] = block.astype(BF16)
     for s in range(slots, padded):
         mix[s] = jnp.zeros((heads, head), F32)
         tot[s] = jnp.zeros((heads, head), F32)
@@ -180,18 +191,22 @@
         mix[s] = jnp.dot(p.astype(BF16), vals[s], preferred_element_type=F32)
         tot[s] = jnp.broadcast_to(jnp.sum(p, axis=1, keepdims=True), (heads, head))
 
+    both = jnp.concatenate(
+        [mix[...].reshape(padded * heads, head), tot[...].reshape(padded * heads, head)], axis=1
+    )
+    hi = both.astype(BF16)
+    lo = (both - hi.astype(F32)).astype(BF16)
+    sums = jnp.dot(adder[...], hi, preferred_element_type=F32)
+    sums = sums + jnp.dot(adder[...], lo, preferred_element_type=F32)
+    value_sum, weight_sum = sums[:, :128], sums[:, 128:]
+    there = weight_sum > 0.0
+    safe = jnp.where(there, weight_sum, 1.0)
+    norm = (value_sum / safe).reshape(grp_count, heads, head)
+    lse = jnp.where(there, group_max[...].reshape(grp_count * heads, 128) + jnp.log2(safe), NEG)
+    norm_f[...] = lse.reshape(grp_count, heads, head)
     stat = jnp.full((grp_count, 128), NEG, F32)
     for h in range(heads):
-        both = jnp.concatenate([mix[:, h, :], tot[:, h, :]], axis=1)
-        hi = both.astype(BF16)
-        lo = (both - hi.astype(F32)).astype(BF16)
-        sums = jnp.dot(onehot2, jnp.concatenate([hi, lo], axis=0), preferred_element_type=F32)
-        value_sum, weight_sum = sums[:, :128], sums[:, 128:]
-        there = weight_sum > 0.0
-        safe = jnp.where(there, weight_sum, 1.0)
-        norm_f[:, h, :] = value_sum / safe
-        lse = jnp.where(there, group_max[:, h, :] + jnp.log2(safe), NEG)
-        stat = jnp.where(lane_r == h, lse, stat)
+        stat = jnp.where(lane_r == h, norm_f[:, h, :], stat)
     other = jnp.concatenate([stat[grp_count // 2 :], stat[: grp_count // 2]], axis=0)
     other = jnp.where(
         lax.rem(row, 4) < 2, pltpu.roll(other, grp_count - 2, 0), pltpu.roll(other, 2, 0)
@@ -199,7 +214,7 @@
     stat = jnp.where((lane_r >= heads) & (lane_r < 2 * heads), pltpu.roll(other, heads, 1), stat)
     stat_out[:, 0, :] = stat
     for r in range(grp_count):
-        msg[r] = jnp.concatenate([norm_f[r], norm_f[r ^ 18]], axis=0).astype(BF16)
+        msg[r] = jnp.concatenate([norm[r], norm[r ^ 18]], axis=0).astype(BF16)
     got[g] = msg[g]
     stat_in[g] = stat_out[g]
     for _, dz, dy in OFFSETS:
@@ -217,16 +232,23 @@
         [share[:, r : r + 1] * got[r].astype(F32) for r in range(grp_count)]
     ).astype(BF16)
 
-    for _, dz, dy in NEAR:
-        push(att.at[g], att.at[g], 3, {"grp": grp_at(dz, dy)})
+    for far, dz, dy in NEAR:
+        push(att.at[g], att.at[g], 3 if far == 3 else 5, {"grp": grp_at(dz, dy)})
     big[2].wait()
-    await_bytes(att, len(NEAR), recv_sems.at[3])
-
-    for dz, dy in [(0, 0)] + [(dz, dy) for _, dz, dy in NEAR]:
-        home = grp_at(Z - dz, Y - dy)
-        both = att[home].astype(F32)
-        att_f[home] = both[:heads]
-        att_f[grp_at(Z - dz + Z // 2, Y - dy + Y // 2)] = both[heads:]
+
+    def unpack(offsets):
+        for dz, dy in offsets:
+            home = grp_at(Z - dz, Y - dy)
+            both = att[home].astype(F32)
+            att_f[home] = both[:heads]
+            att_f[grp_at(Z - dz + Z // 2, Y - dy + Y // 2)] = both[heads:]
+
+    closer = [(dz, dy) for far, dz, dy in NEAR if far < 3]
+    farthest = [(dz, dy) for far, dz, dy in NEAR if far == 3]
+    await_bytes(att, len(closer), recv_sems.at[5])
+    unpack([(0, 0)] + closer)
+    await_bytes(att, len(farthest), recv_sems.at[3])
+    unpack(farthest)
     flat = jnp.concatenate([att_f[:, h, :] for h in range(heads)], axis=1).astype(BF16)
     part = jnp.dot(flat, w[...], preferred_element_type=F32)
 
@@ -245,17 +267,17 @@
     part_in[t] = part_out[t]
     for i in tp_order:
         push(part_out.at[tp_peer(i)], part_in.at[t], 4, {"tp": tp_peer(i)})
+    await_bytes(q_all, grp_count - 1, send_sems.at[0])
+    await_bytes(msg, grp_count - 1, send_sems.at[1])
+    await_bytes(stat_out, grp_count - 1, send_sems.at[2])
+    await_bytes(att, len(farthest), send_sems.at[3])
+    await_bytes(att, len(closer), send_sems.at[5])
+    await_bytes(part_out, tp_count - 1, send_sems.at[4])
     await_bytes(part_in, tp_count - 1, recv_sems.at[4])
     tile = tree([part_in[p] for p in range(tp_count)])
     out_ref[...] = jnp.concatenate(
         [tile[:, width * j : width * (j + 1)] for j in range(rows)], axis=0
     ).astype(BF16)
-
-    await_bytes(q_all, grp_count - 1, send_sems.at[0])
-    await_bytes(msg, grp_count - 1, send_sems.at[1])
-    await_bytes(stat_out, grp_count - 1, send_sems.at[2])
-    await_bytes(att, len(NEAR), send_sems.at[3])
-    await_bytes(part_out, tp_count - 1, send_sems.at[4])
 
 
 def body(
@@ -286,6 +308,7 @@
             pltpu.VMEM((padded, heads, head), F32),
             pltpu.VMEM((padded, heads, head), F32),
             pltpu.VMEM((requests, heads, head), F32),
+            pltpu.VMEM((requests * heads, padded * heads), BF16),
             pltpu.VMEM((requests, 2 * heads, head), BF16),
             pltpu.VMEM((requests, 2 * heads, head), BF16),
             pltpu.VMEM((requests, 1, 128), F32),
@@ -298,8 +321,8 @@
             pltpu.SemaphoreType.DMA,
             pltpu.SemaphoreType.DMA,
             pltpu.SemaphoreType.DMA,
-            pltpu.SemaphoreType.DMA((5,)),
-            pltpu.SemaphoreType.DMA((5,)),
+            pltpu.SemaphoreType.DMA((6,)),
+            pltpu.SemaphoreType.DMA((6,)),
         ],
         compiler_params=pltpu.CompilerParams(
             collective_id=0, has_side_effects=True, vmem_limit_bytes=32 << 20

time: 35.4 us -> 35.1 us (level)
  no operation moved by 1% of the time
where the time goes in v4:
time: 35.1 us; the launch traced here: 35 us
  Pallas kernels  34.4 us (98%)
  local copies, waits for them, and re-layouts  0.6 us (2%)
    pallas_call x1, Pallas kernels, body(): pl.pallas_call(functools.partial(kernel, grp_count, tp_count), out_shape=...  34.4 us

profile of v4, /device:TPU:1, one launch (start us, length us, event | category | flops | bytes accessed | tf_op | source)
XLA Modules:
  0.0 35.0 jit_solution(13733717506847343098)
XLA Ops:
  0.0 34.4 %shard_map.82 = bf16[32,32]{1,0:T(8,128)(2,1)S(1)} custom-call(bf16[1,8,128]{2,1,0:T(8,128)(2,1)} %q_hbm.1, bf16[1,1,128]{2,1,0:T(2,128)(2,1)} %nk_hbm.1, bf16[1,1,128]{2,1,0:T(2,128)(2,1)} %nv_hbm.1, bf16[96,256,128]{2,1,0:T(8,128)(2,1)} %bitcast.3, bf16[96,256,128]{2,1,0:T(8,128)(2,1)} %bitcast.4, s32[32]{0:T(128)} %len_hbm.1, s32[2,96]{1,0:T(2,128)} %bitcast.5, ...), custom_call_target="tpu_custom_call" | custom-call | tf_op jit(solution)/shard_map/pallas_call | solution.py:291
  34.4 0.6 %copy.10 = bf16[32,32]{1,0:T(8,128)(2,1)} copy(bf16[32,32]{1,0:T(8,128)(2,1)S(1)} %shard_map.82) | data formatting | bytes 4096
